TPU v7x, 256 devices: a whole 4x4x8 slice. The times are simulated.
256 devices in a mesh: grp: 8 (over z_hi, core), tile: 32 (over x, y, z_lo).
Axes of the slice: x: 4, y: 4, z: 8 (z_hi: 4, z_lo: 2; z = z_hi * 2 + z_lo), core: 2. Of those that a mesh axis runs over, the one named last changes fastest.
Arguments:
- right_side: float32 [256, 16384], P('grp', 'tile'), may hold values from -8 to 8
- diagonal: float32 [256, 16384], P('grp', 'tile'), may hold values from 0.25 to 2
- inverse_factor: float32 [16384, 16384], P(('grp', 'tile')), may hold values from -2 to 2, as said below
Outputs:
- solution_field: float32 [256, 16384], P('grp', 'tile')
Inputs may be any that keep to these rules, and one draw needn't show every extreme that they name: `inverse_factor`: zero above the diagonal; the diagonal lies between 1 and 2.
All inputs are finite; a program needn't handle non-finite values.
Results may differ from a plain program's by a relative error of at most 0.0003.
Values sent between devices are 32-bit elements; how exact they have to be, the bound alone decides.
A program may use at most 64 MiB of HBM per device.

v0:
```python
import jax
import jax.numpy as jnp
from jax import lax
from jax.sharding import PartitionSpec as P

FAC = 16
SWEEPS = 4
CYCLES = 2


def extended(block, sides, width):
    for axis, dim in sides:
        count = lax.axis_size(axis)
        forward = [(i, i + 1) for i in range(count - 1)]
        backward = [(target, source) for source, target in forward]
        low = lax.ppermute(
            lax.slice_in_dim(block, block.shape[dim] - width, None, axis=dim), axis, forward
        )
        high = lax.ppermute(lax.slice_in_dim(block, 0, width, axis=dim), axis, backward)
        block = jnp.concatenate([low, block, high], axis=dim)
    return block


def operate(field, diagonal):
    padded = extended(field, (("grp", 0), ("tile", 1)), 1)
    beside = padded[2:, 1:-1] + padded[:-2, 1:-1] + padded[1:-1, 2:] + padded[1:-1, :-2]
    beside = beside + padded[2:, :-2] + padded[:-2, 2:]
    return (6.0 + diagonal) * field - beside


def shards(right_side, diagonal, inverse_factor):
    rows_here, cols_here = right_side.shape
    coarse_here = inverse_factor.shape[0]
    scale = 1.0 / (6.0 + diagonal)
    solution_field = jnp.zeros_like(right_side)
    for cycle in range(CYCLES):
        if cycle == 0:
            residual = right_side
        else:
            residual = right_side - operate(solution_field, diagonal)
        smoothed = None
        coarse_rhs = jnp.mean(
            residual.reshape(rows_here // FAC, FAC, cols_here // FAC, FAC), axis=(1, 3)
        ).reshape(-1)
        inner = jnp.dot(
            inverse_factor,
            lax.all_gather(coarse_rhs, ("grp", "tile"), axis=0, tiled=True),
            precision=lax.Precision.HIGHEST,
        )
        smoothed = 0.8 * residual * scale
        for sweep in range(SWEEPS - 1):
            smoothed = smoothed + 0.8 * (residual - operate(smoothed, diagonal)) * scale
        whole_term = jnp.dot(inner, inverse_factor, precision=lax.Precision.HIGHEST)
        summed = lax.psum(whole_term, ("grp", "tile"))
        offset = lax.axis_index(("grp", "tile")) * coarse_here
        coarse_fix = lax.dynamic_slice_in_dim(summed, offset, coarse_here, 0)
        blocks = coarse_fix.reshape(rows_here // FAC, 1, cols_here // FAC, 1)
        spread_fix = jnp.broadcast_to(
            blocks, (rows_here // FAC, FAC, cols_here // FAC, FAC)
        ).reshape(rows_here, cols_here)
        solution_field = solution_field + smoothed + 0.5 * spread_fix
    return solution_field


def solution(mesh):
    placed = (P("grp", "tile"), P("grp", "tile"), P(("grp", "tile"), None))
    return jax.shard_map(
        shards, mesh=mesh, in_specs=placed, out_specs=P("grp", "tile"), check_vma=False
    )
```

profile of v0, /device:TPU:1, one launch (start us, length us, event | category | flops | bytes accessed | tf_op | source)
XLA Modules:
  0.0 1096.1 jit_solution(2937678232551976307)
XLA Ops:
  7.4 5.1 collective-permute-start
  12.6 3.1 collective-permute-start.1
  16.5 3.5 collective-permute-start.3
  21.3 3.2 collective-permute-done.2
  25.6 1.9 collective-permute-start.4
  27.6 6.5 collective-permute-start.5
  35.2 3.7 collective-permute-start.7
  40.4 3.1 collective-permute-done.6
  44.6 1.9 collective-permute-start.8
  46.5 6.2 collective-permute-start.9
  53.8 3.5 collective-permute-start.11
  58.6 239.1 %all-reduce.11.cloned.1.call-done = f32[16384]{0:T(1024)} async-done(((f32[16384]{0:T(1024)}), f32[16384]{0:T(1024)}) %all-reduce.11.cloned.1.call-update) | async-done | bytes 65552
  297.8 5.7 convolution_bitcast_fusion.1
  303.5 2.7 fusion.50
  306.4 234.0 %all-reduce.7.cloned.1.call-done = f32[16384]{0:T(1024)} async-done(((f32[16384]{0:T(1024)}), f32[16384]{0:T(1024)}) %all-reduce.7.cloned.1.call-update) | async-done | bytes 65552 | tf_op jit(solution)/shard_map/psum | solution.py:54
  541.8 1.9 collective-permute-start.12
  543.7 4.5 collective-permute-start.13
  549.1 3.7 collective-permute-start.15
  554.0 3.2 collective-permute-done.14
  557.5 1.9 collective-permute-start.16
  559.4 6.5 collective-permute-start.17
  566.7 2.8 collective-permute-start.19
  570.8 3.2 collective-permute-done.18
  576.2 6.5 collective-permute-start.21
  583.5 3.5 collective-permute-start.23
  588.5 3.1 collective-permute-done.22
  593.7 6.6 collective-permute-start.25
  601.5 3.1 collective-permute-start.27
  606.1 238.9 %all-reduce.13.cloned.1.call-done = f32[16384]{0:T(1024)} async-done(((f32[16384]{0:T(1024)}), f32[16384]{0:T(1024)}) %all-reduce.13.cloned.1.call-update) | async-done | bytes 65552
  844.9 5.7 convolution_bitcast_fusion
  850.6 2.7 fusion.51
  853.5 234.1 %all-reduce.9.cloned.1.call-done = f32[16384]{0:T(1024)} async-done(((f32[16384]{0:T(1024)}), f32[16384]{0:T(1024)}) %all-reduce.9.cloned.1.call-update) | async-done | bytes 65552 | tf_op jit(solution)/shard_map/psum | solution.py:54
  (101 shorter events, 27.1 us)
Async XLA Ops:
  6.5 291.2 %all-reduce.11.cloned.1.call-start = ((), (), s32[]{:S(2)}) async-start(), calls=%async_computation.2 | async-start | bytes 131072
  7.4 8.2 collective-permute-start
  12.6 3.8 collective-permute-start.1
  16.5 4.8 collective-permute-start.3
  20.0 4.5 collective-permute-start.2
  25.6 9.5 collective-permute-start.4
  27.6 7.6 collective-permute-start.5
  35.2 5.1 collective-permute-start.7
  38.9 4.5 collective-permute-start.6
  44.6 9.1 collective-permute-start.8
  46.5 7.2 collective-permute-start.9
  53.7 486.7 %all-reduce.7.cloned.1.call-start = ((), (), s32[]{:S(2)}) async-start(), calls=%async_computation | async-start | bytes 131072 | tf_op jit(solution)/shard_map/psum | solution.py:54
  53.8 252.4 %collective-permute-start.11 = (f32[34,1]{1,0:T(8,128)S(1)}, f32[34,1]{1,0:T(8,128)S(1)}, u32[]{:S(2)}, u32[]{:S(2)}) collective-permute-start(f32[34,1]{1,0:T(8,128)S(1)} %get-tuple-element.25), channel_id=1, source_target_pairs={{0,1},{1,2},{2,3},{3,4},{4,5},{5,6},{6,7},{7,8},{8,9},{9,10},{10,1... | collective-permute-start | bytes 416 | tf_op jit(solution)/shard_map/ppermute | solution.py:16
  57.3 249.0 %collective-permute-start.10 = (f32[34,1]{1,0:T(8,128)S(1)}, f32[34,1]{1,0:T(8,128)S(1)}, u32[]{:S(2)}, u32[]{:S(2)}) collective-permute-start(f32[34,1]{1,0:T(8,128)S(1)} %get-tuple-element.26), channel_id=1, source_target_pairs={{1,0},{2,1},{3,2},{4,3},{5,4},{6,5},{7,6},{8,7},{9,8},{10,9},{11,1... | collective-permute-start | bytes 416 | tf_op jit(solution)/shard_map/ppermute | solution.py:19
  306.2 538.7 %all-reduce.13.cloned.1.call-start = ((), (), s32[]{:S(2)}) async-start(), calls=%async_computation.3 | async-start | bytes 131072
  541.8 6.5 collective-permute-start.12
  543.7 5.3 collective-permute-start.13
  549.1 5.0 collective-permute-start.15
  552.7 4.5 collective-permute-start.14
  557.5 8.5 collective-permute-start.16
  559.4 7.2 collective-permute-start.17
  566.7 4.1 collective-permute-start.19
  569.5 4.5 collective-permute-start.18
  574.3 8.7 collective-permute-start.20
  576.2 7.2 collective-permute-start.21
  583.5 5.0 collective-permute-start.23
  587.0 4.5 collective-permute-start.22
  591.8 9.6 collective-permute-start.24
  593.7 7.7 collective-permute-start.25
  601.4 486.2 %all-reduce.9.cloned.1.call-start = ((), (), s32[]{:S(2)}) async-start(), calls=%async_computation.1 | async-start | bytes 131072 | tf_op jit(solution)/shard_map/psum | solution.py:54
  601.5 251.9 %collective-permute-start.27 = (f32[34,1]{1,0:T(8,128)S(1)}, f32[34,1]{1,0:T(8,128)S(1)}, u32[]{:S(2)}, u32[]{:S(2)}) collective-permute-start(f32[34,1]{1,0:T(8,128)S(1)} %get-tuple-element.9), channel_id=1, source_target_pairs={{0,1},{1,2},{2,3},{3,4},{4,5},{5,6},{6,7},{7,8},{8,9},{9,10},{10,1... | collective-permute-start | bytes 416 | tf_op jit(solution)/shard_map/ppermute | solution.py:16
  604.6 248.8 %collective-permute-start.26 = (f32[34,1]{1,0:T(8,128)S(1)}, f32[34,1]{1,0:T(8,128)S(1)}, u32[]{:S(2)}, u32[]{:S(2)}) collective-permute-start(f32[34,1]{1,0:T(8,128)S(1)} %get-tuple-element.10), channel_id=1, source_target_pairs={{1,0},{2,1},{3,2},{4,3},{5,4},{6,5},{7,6},{8,7},{9,8},{10,9},{11,1... | collective-permute-start | bytes 416 | tf_op jit(solution)/shard_map/ppermute | solution.py:19
  (6 other events, 500.5 us)
Sparse Core Ops, SparseCore 0:
  53.8 243.9 all-reduce.10
  306.3 234.0 all-reduce.6
  601.5 243.4 all-reduce.12
  853.5 234.0 all-reduce.8
where the time goes:
time: 1100 us
  waiting for transfers between devices  965 us (88%)
  starting transfers between devices  89.7 us (8%)
  matrix products  16.9 us (2%)
  between operations  13.7 us (1%)
    unnamed x6, waiting for transfers between devices  478 us
    psum x2, waiting for transfers between devices, shards(): summed = lax.psum(whole_term, ('grp', 'tile'))  468 us
    ppermute x14, starting transfers between devices, extended(): lax.ppermute(lax.slice_in_dim(block, block.shape[dim] - width, None, axis...  63.7 us
    ppermute x14, starting transfers between devices, extended(): lax.ppermute(lax.slice_in_dim(block, 0, width, axis=dim), axis, backward)  25.9 us
  transfers between devices with their start and end apart: 32, of which 13 were waited for; matrix products, arithmetic and copies ran while one was open for 2% of the time, Pallas kernels for 0%

commit v1 on v0

--- a/solution.py
+++ b/solution.py
@@ -51,7 +51,7 @@
         for sweep in range(SWEEPS - 1):
             smoothed = smoothed + 0.8 * (residual - operate(smoothed, diagonal)) * scale
         whole_term = jnp.dot(inner, inverse_factor, precision=lax.Precision.HIGHEST)
-        summed = lax.psum(whole_term, ("grp", "tile"))
+        summed = lax.psum(lax.psum(whole_term, "tile"), "grp")
         offset = lax.axis_index(("grp", "tile")) * coarse_here
         coarse_fix = lax.dynamic_slice_in_dim(summed, offset, coarse_here, 0)
         blocks = coarse_fix.reshape(rows_here // FAC, 1, cols_here // FAC, 1)

time: 1100 us -> 1290 us (1.17)
  waiting for transfers between devices: 965 us -> 1160 us
    psum x2 -> x4, waiting for transfers between devices: 468 us -> 676 us  [shards(): summed = lax.psum(lax.psum(whole_term, 'tile'), 'grp')]
    unnamed x6 -> x8, waiting for transfers between devices: 478 us -> 462 us
  transfers between devices with their start and end apart: 32 -> 34, of which waited for: 13 -> 14; matrix products, arithmetic and copies ran while one was open for 2% -> 2% of each run, Pallas kernels for 0% -> 0%
where the time goes in v1:
time: 1290 us
  waiting for transfers between devices  1160 us (90%)
  starting transfers between devices  88.6 us (7%)
  matrix products  16.9 us (1%)
  between operations  14.1 us (1%)
    psum x4, waiting for transfers between devices, shards(): summed = lax.psum(lax.psum(whole_term, 'tile'), 'grp')  676 us
    unnamed x8, waiting for transfers between devices  462 us
    ppermute x14, starting transfers between devices, extended(): lax.ppermute(lax.slice_in_dim(block, block.shape[dim] - width, None, axis...  60.6 us
    ppermute x14, starting transfers between devices, extended(): lax.ppermute(lax.slice_in_dim(block, 0, width, axis=dim), axis, backward)  27.8 us
  transfers between devices with their start and end apart: 34, of which 14 were waited for; matrix products, arithmetic and copies ran while one was open for 2% of the time, Pallas kernels for 0%

profile of v1, /device:TPU:1, one launch (start us, length us, event | category | flops | bytes accessed | tf_op | source)
XLA Modules:
  0.0 1286.7 jit_solution(341953424890711361)
XLA Ops:
  7.4 5.1 collective-permute-start
  12.6 3.1 collective-permute-start.1
  16.8 3.5 collective-permute-start.3
  21.8 3.1 collective-permute-done.2
  27.9 6.3 collective-permute-start.5
  35.4 3.5 collective-permute-start.7
  40.2 3.2 collective-permute-done.6
  46.5 6.1 collective-permute-start.9
  52.6 224.2 %all-reduce.17.cloned.1.call-done = f32[16384]{0:T(1024)} async-done(((f32[16384]{0:T(1024)}), f32[16384]{0:T(1024)}) %all-reduce.17.cloned.1.call-update) | async-done | bytes 65552
  276.8 5.7 convolution_bitcast_fusion.1
  282.5 2.7 fusion.50
  285.4 3.7 collective-permute-start.11
  290.3 252.7 %all-reduce.9.cloned.1.call-done = f32[16384]{0:T(1024)} async-done(((f32[16384]{0:T(1024)}), f32[16384]{0:T(1024)}) %all-reduce.9.cloned.1.call-update) | async-done | bytes 65552 | tf_op jit(solution)/shard_map/psum | solution.py:54
  543.3 85.5 %all-reduce.11.cloned.1.call-done = f32[16384]{0:T(1024)} async-done(((f32[16384]{0:T(1024)}), f32[16384]{0:T(1024)}) %all-reduce.11.cloned.1.call-update) | async-done | bytes 65552 | tf_op jit(solution)/shard_map/psum | solution.py:54
  630.2 3.6 collective-permute-start.12
  633.7 2.9 collective-permute-start.13
  637.4 2.3 collective-permute-start.15
  641.0 4.2 collective-permute-done.14
  645.5 2.4 collective-permute-start.16
  647.9 5.3 collective-permute-start.17
  654.0 4.5 collective-permute-start.19
  660.0 3.1 collective-permute-done.18
  665.2 6.5 collective-permute-start.21
  672.5 2.7 collective-permute-start.23
  676.6 3.3 collective-permute-done.22
  682.1 6.5 collective-permute-start.25
  688.6 237.4 %all-reduce.19.cloned.1.call-done = f32[16384]{0:T(1024)} async-done(((f32[16384]{0:T(1024)}), f32[16384]{0:T(1024)}) %all-reduce.19.cloned.1.call-update) | async-done | bytes 65552
  926.1 5.7 convolution_bitcast_fusion
  931.8 2.7 fusion.51
  934.7 3.7 collective-permute-start.27
  939.6 252.7 %all-reduce.13.cloned.1.call-done = f32[16384]{0:T(1024)} async-done(((f32[16384]{0:T(1024)}), f32[16384]{0:T(1024)}) %all-reduce.13.cloned.1.call-update) | async-done | bytes 65552 | tf_op jit(solution)/shard_map/psum | solution.py:54
  1192.5 85.4 %all-reduce.15.cloned.1.call-done = f32[16384]{0:T(1024)} async-done(((f32[16384]{0:T(1024)}), f32[16384]{0:T(1024)}) %all-reduce.15.cloned.1.call-update) | async-done | bytes 65552 | tf_op jit(solution)/shard_map/psum | solution.py:54
  (107 shorter events, 29.2 us)
Async XLA Ops:
  6.5 270.2 %all-reduce.17.cloned.1.call-start = ((), (), s32[]{:S(2)}) async-start(), calls=%async_computation.4 | async-start | bytes 131072
  7.4 9.3 collective-permute-start
  12.6 4.1 collective-permute-start.1
  16.8 5.0 collective-permute-start.3
  20.4 4.5 collective-permute-start.2
  26.0 9.3 collective-permute-start.4
  27.9 7.4 collective-permute-start.5
  35.2 507.8 %all-reduce.9.cloned.1.call-start = ((), (), s32[]{:S(2)}) async-start(), calls=%async_computation | async-start | bytes 131072 | tf_op jit(solution)/shard_map/psum | solution.py:54
  35.4 4.8 collective-permute-start.7
  38.9 4.5 collective-permute-start.6
  44.5 240.7 %collective-permute-start.8 = (f32[1,512]{1,0:T(1,128)S(1)}, f32[1,512]{1,0:T(1,128)S(1)}, u32[]{:S(2)}, u32[]{:S(2)}) collective-permute-start(f32[1,512]{1,0:T(1,128)S(1)} %get-tuple-element.44), channel_id=1, source_target_pairs={{32,0},{64,32},{96,64},{128,96},{160,128},{192,160},{224,192},{33,... | collective-permute-start | bytes 6152 | tf_op jit(solution)/shard_map/ppermute | solution.py:19
  46.5 238.8 %collective-permute-start.9 = (f32[1,512]{1,0:T(1,128)S(1)}, f32[1,512]{1,0:T(1,128)S(1)}, u32[]{:S(2)}, u32[]{:S(2)}) collective-permute-start(f32[1,512]{1,0:T(1,128)S(1)} %get-tuple-element.43), channel_id=1, source_target_pairs={{0,32},{32,64},{64,96},{96,128},{128,160},{160,192},{192,224},{1,3... | collective-permute-start | bytes 6152 | tf_op jit(solution)/shard_map/ppermute | solution.py:16
  285.2 343.6 %all-reduce.11.cloned.1.call-start = ((), (), s32[]{:S(2)}) async-start(), calls=%async_computation.1 | async-start | bytes 131072 | tf_op jit(solution)/shard_map/psum | solution.py:54
  285.4 257.8 %collective-permute-start.11 = (f32[34,1]{1,0:T(8,128)S(1)}, f32[34,1]{1,0:T(8,128)S(1)}, u32[]{:S(2)}, u32[]{:S(2)}) collective-permute-start(f32[34,1]{1,0:T(8,128)S(1)} %get-tuple-element.25), channel_id=1, source_target_pairs={{0,1},{1,2},{2,3},{3,4},{4,5},{5,6},{6,7},{7,8},{8,9},{9,10},{10,1... | collective-permute-start | bytes 416 | tf_op jit(solution)/shard_map/ppermute | solution.py:16
  289.0 254.1 %collective-permute-start.10 = (f32[34,1]{1,0:T(8,128)S(1)}, f32[34,1]{1,0:T(8,128)S(1)}, u32[]{:S(2)}, u32[]{:S(2)}) collective-permute-start(f32[34,1]{1,0:T(8,128)S(1)} %get-tuple-element.26), channel_id=1, source_target_pairs={{1,0},{2,1},{3,2},{4,3},{5,4},{6,5},{7,6},{8,7},{9,8},{10,9},{11,1... | collective-permute-start | bytes 416 | tf_op jit(solution)/shard_map/ppermute | solution.py:19
  543.1 383.0 %all-reduce.19.cloned.1.call-start = ((), (), s32[]{:S(2)}) async-start(), calls=%async_computation.5 | async-start | bytes 131072
  630.2 6.5 collective-permute-start.12
  639.7 5.5 collective-permute-start.14
  645.5 7.9 collective-permute-start.16
  647.9 6.1 collective-permute-start.17
  654.0 6.0 collective-permute-start.19
  658.5 4.5 collective-permute-start.18
  663.3 8.8 collective-permute-start.20
  665.2 7.2 collective-permute-start.21
  672.5 4.1 collective-permute-start.23
  675.2 4.7 collective-permute-start.22
  676.6 515.8 %all-reduce.13.cloned.1.call-start = ((), (), s32[]{:S(2)}) async-start(), calls=%async_computation.2 | async-start | bytes 131072 | tf_op jit(solution)/shard_map/psum | solution.py:54
  680.2 254.4 %collective-permute-start.24 = (f32[1,512]{1,0:T(1,128)S(1)}, f32[1,512]{1,0:T(1,128)S(1)}, u32[]{:S(2)}, u32[]{:S(2)}) collective-permute-start(f32[1,512]{1,0:T(1,128)S(1)} %get-tuple-element.36), channel_id=1, source_target_pairs={{32,0},{64,32},{96,64},{128,96},{160,128},{192,160},{224,192},{33,... | collective-permute-start | bytes 6152 | tf_op jit(solution)/shard_map/ppermute | solution.py:19
  682.1 252.5 %collective-permute-start.25 = (f32[1,512]{1,0:T(1,128)S(1)}, f32[1,512]{1,0:T(1,128)S(1)}, u32[]{:S(2)}, u32[]{:S(2)}) collective-permute-start(f32[1,512]{1,0:T(1,128)S(1)} %get-tuple-element.35), channel_id=1, source_target_pairs={{0,32},{32,64},{64,96},{96,128},{128,160},{160,192},{192,224},{1,3... | collective-permute-start | bytes 6152 | tf_op jit(solution)/shard_map/ppermute | solution.py:16
  934.5 343.4 %all-reduce.15.cloned.1.call-start = ((), (), s32[]{:S(2)}) async-start(), calls=%async_computation.3 | async-start | bytes 131072 | tf_op jit(solution)/shard_map/psum | solution.py:54
  934.7 257.7 %collective-permute-start.27 = (f32[34,1]{1,0:T(8,128)S(1)}, f32[34,1]{1,0:T(8,128)S(1)}, u32[]{:S(2)}, u32[]{:S(2)}) collective-permute-start(f32[34,1]{1,0:T(8,128)S(1)} %get-tuple-element.9), channel_id=1, source_target_pairs={{0,1},{1,2},{2,3},{3,4},{4,5},{5,6},{6,7},{7,8},{8,9},{9,10},{10,1... | collective-permute-start | bytes 416 | tf_op jit(solution)/shard_map/ppermute | solution.py:16
  938.3 254.1 %collective-permute-start.26 = (f32[34,1]{1,0:T(8,128)S(1)}, f32[34,1]{1,0:T(8,128)S(1)}, u32[]{:S(2)}, u32[]{:S(2)}) collective-permute-start(f32[34,1]{1,0:T(8,128)S(1)} %get-tuple-element.10), channel_id=1, source_target_pairs={{1,0},{2,1},{3,2},{4,3},{5,4},{6,5},{7,6},{8,7},{9,8},{10,9},{11,1... | collective-permute-start | bytes 416 | tf_op jit(solution)/shard_map/ppermute | solution.py:19
  (8 other events, 730.2 us)
Sparse Core Ops, SparseCore 0:
  35.4 241.3 all-reduce.16
  285.3 257.6 all-reduce.8
  545.9 82.8 all-reduce.10
  676.7 249.3 all-reduce.18
  934.6 257.6 all-reduce.12
  1195.0 82.8 all-reduce.14
